TPU v7x, 32 devices: a whole 2x2x4 slice. The times are simulated.
32 devices in a mesh: space: 8 (over y, x, core), dp: 4 (over z).
Axes of the slice: x: 2, y: 2, z: 4, core: 2. Of those that a mesh axis runs over, the one named last changes fastest.
Arguments:
- volume: bfloat16 [256, 96, 8, 128], P(('dp', 'space')), parts along dimension 0, may hold values from -6 to 6
- kernel: bfloat16 [96, 2592], replicated, may hold values from -0.125 to 0.125
- beta: float32 [96], replicated, may hold values from 0.5 to 2
- gamma: float32 [96, 96], replicated, may hold values from 0 to 0.04
- cotangent: bfloat16 [32, 96, 8, 128], P(('dp', 'space')), parts along dimension 0, may hold values from -6 to 6
Outputs:
- normalized: bfloat16 [32, 96, 8, 128], P(('dp', 'space')), parts along dimension 0
- volume_input_gradient: bfloat16 [256, 96, 8, 128], P(('dp', 'space')), parts along dimension 0
- kernel_grad: float32 [384, 2592], P('dp'), parts along dimension 0
- gamma_grad: float32 [384, 96], P('dp'), parts along dimension 0
- beta_grad: float32 [384], P('dp'), parts along dimension 0
There are 4 independent parts, one for each index of `dp`. A program takes and returns all parts, laid end to end along the dimension named above; an argument that names none is the same for every part. Nothing has to cross between parts.
All inputs are finite; a program needn't handle non-finite values.
Results may differ from a plain program's by a relative error of at most 0.0049.
Values may be sent and summed in bfloat16 or wider, within the bound.
A program may use at most 64 MiB of HBM per device.

v0:
```python
import math

import jax
import jax.numpy as jnp
from jax import lax
from jax.sharding import PartitionSpec as P

BLOCK_OUTPUT_Z = 16


def from_behind(value, axis, steps):
    count = lax.axis_size(axis)
    leading, last = (max(0, -steps), min(count, count - steps))
    return lax.ppermute(value, axis, [(source, source + steps) for source in range(leading, last)])


def pull_lower(field, axis_num, sender, usable, span_z):
    if axis_num == 0:
        sliver = field[..., -1:, :]
        arrived = sender(sliver, 8)
        arrived = jnp.where(usable, arrived, jnp.zeros_like(arrived))
        return jnp.concatenate([arrived, field[..., :-1, :]], axis=field.ndim - 2)
    if axis_num == 1:
        sliver = field[..., -span_z:]
        arrived = sender(sliver, 2)
        arrived = jnp.where(usable, arrived, jnp.zeros_like(arrived))
        return jnp.concatenate([arrived, field[..., :-span_z]], axis=field.ndim - 1)
    sliver = field[..., span_z - 1 :: span_z]
    arrived = sender(sliver, 1)
    arrived = jnp.where(usable, arrived, jnp.zeros_like(arrived))
    rolled = jnp.concatenate([jnp.zeros_like(field[..., :1]), field[..., :-1]], axis=field.ndim - 1)
    spread = jnp.repeat(arrived, span_z, axis=field.ndim - 1)
    lanes = lax.broadcasted_iota(jnp.int32, field.shape, field.ndim - 1) % span_z
    return jnp.where(lanes == 0, spread, rolled)


def pull_upper(field, axis_num, sender, usable, span_z):
    if axis_num == 0:
        sliver = field[..., :1, :]
        arrived = sender(sliver, -8)
        arrived = jnp.where(usable, arrived, jnp.zeros_like(arrived))
        return jnp.concatenate([field[..., 1:, :], arrived], axis=field.ndim - 2)
    if axis_num == 1:
        sliver = field[..., :span_z]
        arrived = sender(sliver, -2)
        arrived = jnp.where(usable, arrived, jnp.zeros_like(arrived))
        return jnp.concatenate([field[..., span_z:], arrived], axis=field.ndim - 1)
    sliver = field[..., 0::span_z]
    arrived = sender(sliver, -1)
    arrived = jnp.where(usable, arrived, jnp.zeros_like(arrived))
    rolled = jnp.concatenate([field[..., 1:], jnp.zeros_like(field[..., :1])], axis=field.ndim - 1)
    spread = jnp.repeat(arrived, span_z, axis=field.ndim - 1)
    lanes = lax.broadcasted_iota(jnp.int32, field.shape, field.ndim - 1) % span_z
    return jnp.where(lanes == span_z - 1, spread, rolled)


def parity_range(shift_flag):
    return slice(0, 2) if shift_flag == 0 else slice(1, 2)


def forward_taps(shift_flag):
    return slice(0, 2) if shift_flag == 0 else slice(2, 3)


def grad_range(parity_flag):
    return slice(0, 1) if parity_flag == 0 else slice(0, 2)


def backward_taps(parity_flag):
    return slice(0, 1) if parity_flag == 0 else slice(1, 3)


def shards(volume, kernel, beta, gamma, cotangent):
    highest = lax.Precision.HIGHEST
    width = kernel.shape[0]
    span_z = BLOCK_OUTPUT_Z
    devices = lax.axis_size("space")
    index = lax.axis_index("space")
    position = (index // 8, index // 2 % 4, index % 2)
    limits = (devices // 8, 4, 2)
    lower_ok = [position[axis_num] > 0 for axis_num in range(3)]
    upper_ok = [position[axis_num] < limits[axis_num] - 1 for axis_num in range(3)]
    rows_x = volume.shape[2]
    lanes_total = volume.shape[3]
    cells = rows_x * lanes_total
    stacked_input = volume.reshape(2, 2, 2, width, rows_x, lanes_total)
    kernel_five = kernel.reshape(width, 3, 3, 3, width)
    reorder = jnp.array([1, 2, 0], jnp.int32)
    kernel_perm = jnp.take(
        jnp.take(jnp.take(kernel_five, reorder, axis=1), reorder, axis=2), reorder, axis=3
    )
    flags = [
        (shift_x, shift_y, shift_z)
        for shift_x in range(2)
        for shift_y in range(2)
        for shift_z in range(2)
    ]
    partial_value = {}
    for pattern in flags:
        weights_sel = kernel_perm[
            :, forward_taps(pattern[0]), forward_taps(pattern[1]), forward_taps(pattern[2])
        ]
        input_sel = stacked_input[
            parity_range(pattern[0]), parity_range(pattern[1]), parity_range(pattern[2])
        ]
        partial_value[pattern] = jnp.einsum(
            "oabci,abcixl->oxl", weights_sel, input_sel, preferred_element_type=jnp.float32
        )
    send_partial = lambda sliver, offset: from_behind(sliver, "space", offset)
    convolved_output = jnp.zeros((width, rows_x, lanes_total), jnp.float32)
    for pattern in flags:
        term = partial_value[pattern]
        for axis_num in range(3):
            if pattern[axis_num]:
                term = pull_lower(term, axis_num, send_partial, lower_ok[axis_num], span_z)
        convolved_output = convolved_output + term
    squared = convolved_output * convolved_output
    denom = beta[:, None, None] + jnp.einsum("ij,jxl->ixl", gamma, squared, precision=highest)
    reciprocal_norm = lax.rsqrt(denom)
    output = (convolved_output * reciprocal_norm).astype(jnp.bfloat16)
    upstream = cotangent[0].astype(jnp.float32)
    weighted = (
        -0.5 * upstream * convolved_output * reciprocal_norm * reciprocal_norm * reciprocal_norm
    )
    coupled = jnp.einsum("ki,kxl->ixl", gamma, weighted, precision=highest)
    grad_conv = (upstream * reciprocal_norm + 2.0 * convolved_output * coupled).astype(jnp.bfloat16)
    send_grad = lambda sliver, offset: from_behind(sliver, "space", offset)
    variants = []
    for pattern in flags:
        term = grad_conv
        for axis_num in range(3):
            if pattern[axis_num]:
                term = pull_upper(term, axis_num, send_grad, upper_ok[axis_num], span_z)
        variants.append(term)
    shifted_grad = jnp.stack(variants).reshape(2, 2, 2, width, rows_x, lanes_total)
    pieces = []
    for parity in flags:
        weights_sel = kernel_perm[
            :, backward_taps(parity[0]), backward_taps(parity[1]), backward_taps(parity[2])
        ]
        grad_sel = shifted_grad[grad_range(parity[0]), grad_range(parity[1]), grad_range(parity[2])]
        summed = jnp.einsum(
            "oabci,abcoxl->ixl", weights_sel, grad_sel, preferred_element_type=jnp.float32
        )
        pieces.append(summed.astype(jnp.bfloat16))
    volume_input_gradient = jnp.stack(pieces)
    plane_pairs = ((0, 0), (1, 0), (1, 1))

    def kernel_plane(plane_index):
        parity_x, shift_x = plane_pairs[plane_index]
        plane = jnp.zeros((width, 3, 3, width), jnp.float32)
        for shift_y in range(2):
            for shift_z in range(2):
                block = jnp.einsum(
                    "oxl,bcixl->obci",
                    shifted_grad[shift_x, shift_y, shift_z],
                    stacked_input[parity_x, parity_range(shift_y), parity_range(shift_z)],
                    preferred_element_type=jnp.float32,
                )
                plane = plane.at[:, forward_taps(shift_y), forward_taps(shift_z), :].set(block)
        return plane

    scale = 1.0 / math.sqrt(cells * devices)
    gamma_local = jnp.einsum("kxl,jxl->kj", weighted, squared, precision=highest)
    beta_local = jnp.sum(weighted, axis=(1, 2))
    local_kernel = jnp.stack([kernel_plane(plane_index) for plane_index in range(3)], axis=1)
    kernel_sum, gamma_grad, beta_grad = lax.psum((local_kernel, gamma_local, beta_local), "space")
    restore = jnp.array([2, 0, 1], jnp.int32)
    kernel_taps = jnp.take(
        jnp.take(jnp.take(kernel_sum, restore, axis=1), restore, axis=2), restore, axis=3
    )
    kernel_grad = kernel_taps.reshape(width, 27 * width)
    return (
        output[None],
        volume_input_gradient,
        kernel_grad * scale,
        gamma_grad * scale,
        beta_grad * scale,
    )


def solution(mesh):
    placed = (
        P(("dp", "space"), None, None, None),
        P(),
        P(),
        P(),
        P(("dp", "space"), None, None, None),
    )
    return jax.shard_map(
        shards,
        mesh=mesh,
        in_specs=placed,
        out_specs=(
            P(("dp", "space"), None, None, None),
            P(("dp", "space"), None, None, None),
            P("dp", None),
            P("dp", None),
            P("dp"),
        ),
        check_vma=False,
    )
```

profile of v0, /device:TPU:0, one launch (start us, length us, event | category | flops | bytes accessed | tf_op | source)
XLA Modules:
  0.0 277.7 jit_solution(5196118742922122444)
XLA Ops:
  7.9 1.4 copy.170
  19.5 5.6 %collective-permute-start.2 = (f32[96,8,16]{2,0,1:T(8,128)}, f32[96,8,16]{2,0,1:T(8,128)}, u32[]{:S(2)}, u32[]{:S(2)}) collective-permute-start(f32[96,8,16]{2,0,1:T(8,128)} %slice.738), channel_id=1, source_target_pairs={{0,8},{4,12},{8,16},{12,20},{16,24},{20,28},{1,9},{5,13},{9,17},{1... | collective-permute-start | bytes 147464 | tf_op jit(solution)/shard_map/ppermute | solution.py:14
  26.9 1.3 collective-permute-start.5
  28.5 2.6 slice.639
  31.1 2.2 collective-permute-start
  38.8 1.8 slice.760
  40.6 1.7 slice.754
  42.3 1.7 slice.748
  44.0 1.4 slice.743
  48.2 3.1 %collective-permute-start.1 = (f32[96,8,16]{2,0,1:T(8,128)}, f32[96,8,16]{2,0,1:T(8,128)}, u32[]{:S(2)}, u32[]{:S(2)}) collective-permute-start(f32[96,8,16]{2,0,1:T(8,128)} %slice.734), channel_id=1, source_target_pairs={{0,8},{4,12},{8,16},{12,20},{16,24},{20,28},{1,9},{5,13},{9,17},{1... | collective-permute-start | bytes 147464 | tf_op jit(solution)/shard_map/ppermute | solution.py:14
  54.0 2.0 copy.177
  56.0 2.3 fusion.4
  61.3 4.4 %collective-permute-start.10 = (f32[96,8,16]{2,0,1:T(8,128)}, f32[96,8,16]{2,0,1:T(8,128)}, u32[]{:S(2)}, u32[]{:S(2)}) collective-permute-start(f32[96,8,16]{2,0,1:T(8,128)} %slice_maximum_fusion), channel_id=1, source_target_pairs={{0,8},{4,12},{8,16},{12,20},{16,24},{20,28},{1,9},{5,13},{9,17},{1... | collective-permute-start | bytes 147464 | tf_op jit(solution)/shard_map/ppermute | solution.py:14
  66.6 2.1 collective-permute-start.8
  68.7 2.5 slice.649
  71.2 3.5 %collective-permute-start.3 = (f32[96,8,8]{2,0,1:T(8,128)}, f32[96,8,8]{2,0,1:T(8,128)}, u32[]{:S(2)}, u32[]{:S(2)}) collective-permute-start(f32[96,8,8]{2,0,1:T(8,128)} %slice.649), channel_id=1, source_target_pairs={{0,4},{4,8},{8,12},{12,16},{16,20},{20,24},{24,28},{1,5},{5,9},{9,... | collective-permute-start | bytes 73736 | tf_op jit(solution)/shard_map/ppermute | solution.py:14
  74.7 2.5 slice.659
  77.3 1.3 collective-permute-start.6
  82.7 2.0 slice.673
  84.7 14.6 %collective-permute-start.11 = (f32[96,8,8]{2,0,1:T(8,128)S(1)}, f32[96,8,8]{2,0,1:T(8,128)S(1)}, u32[]{:S(2)}, u32[]{:S(2)}) collective-permute-start(f32[96,8,8]{2,0,1:T(8,128)S(1)} %slice.673), channel_id=1, source_target_pairs={{0,4},{4,8},{8,12},{12,16},{16,20},{20,24},{24,28},{1,5},{5,9},{9,... | collective-permute-start | bytes 73736 | tf_op jit(solution)/shard_map/ppermute | solution.py:14
  101.8 2.4 fusion.60
  106.1 28.4 %all-reduce.11 = (f32[96,96]{1,0:T(8,128)S(1)}, f32[96]{0:T(128)S(1)}) all-reduce(f32[96,96]{1,0:T(8,128)S(1)} %convolution_bitcast_fusion.24, f32[96]{0:T(128)S(1)} %get-tuple-element.186), channel_id=1, replica_groups=mesh['space'=8,'dp'=4] {'space'}, use_global_device_ids=true, to_apply=%region_2.3 | all-reduce | flops 9312 | bytes 74496 | tf_op jit(solution)/shard_map/psum | solution.py:167
  135.1 1.8 slice.676
  136.9 1.3 collective-permute-start.12
  140.3 1.5 collective-permute-start.13
  144.6 1.7 constant_dynamic-update-slice_fusion.2
  148.6 1.3 collective-permute-start.17
  149.9 2.8 %slice.684 = bf16[96,8,8]{2,0,1:T(8,128)(2,1)} slice(bf16[96,8,128]{2,0,1:T(8,128)(2,1)} %pad_maximum_fusion.5), slice={[0:96:1], [0:8:1], [0:128:16]} | slice | bytes 24576 | tf_op jit(solution)/shard_map/slice | solution.py:48
  152.7 1.3 collective-permute-start.16
  156.9 1.8 slice.680
  158.7 1.3 collective-permute-start.14
  160.0 1.6 broadcast_select_fusion.11
  163.4 1.8 copy.197
  165.2 1.6 broadcast_select_fusion.12
  168.6 1.8 copy.195
  174.8 1.8 slice.688
  176.5 1.3 collective-permute-start.18
  178.7 3.1 %collective-permute-done.18 = bf16[96,8,8]{2,0,1:T(8,128)(2,1)S(1)} collective-permute-done((bf16[96,8,8]{2,0,1:T(8,128)(2,1)}, bf16[96,8,8]{2,0,1:T(8,128)(2,1)S(1)}, u32[]{:S(2)}, u32[]{:S(2)}) %collective-permute-start.18) | collective-permute-done | bytes 12320 | tf_op jit(solution)/shard_map/ppermute | solution.py:14
  183.1 1.6 convolution_bitcast_fusion.16
  184.8 1.6 convolution_bitcast_fusion.15
  187.8 2.2 fusion.37
  190.6 2.2 fusion.40
  193.3 2.1 fusion.34
  203.9 3.2 %copy.232 = bf16[8,96,8,128]{3,2,1,0:T(8,128)(2,1)} copy(bf16[8,96,8,128]{3,1,2,0:T(8,128)(2,1)} %fusion.28) | data formatting | bytes 3145728
  207.1 55.8 %all-reduce.14.cloned.1.call-done = f32[96,3,3,3,96]{4,0,3,2,1:T(8,128)} async-done(((f32[96,3,3,3,96]{4,0,3,2,1:T(8,128)}), f32[96,3,3,3,96]{4,0,3,2,1:T(8,128)}) %all-reduce.14.cloned.1.call-update) | async-done | bytes 995344 | tf_op jit(solution)/shard_map/psum | solution.py:167
  262.9 2.1 gather_fusion.3
  267.7 1.7 copy.230
  269.5 1.4 copy.233
  (209 shorter events, 70.7 us)
Async XLA Ops:
  7.2 97.1 %copy-start = (f32[96,96]{1,0:T(8,128)S(1)}, f32[96,96]{1,0:T(8,128)}, u32[]{:S(2)}) copy-start(f32[96,96]{1,0:T(8,128)} %param.34) | copy-start | bytes 110596
  7.2 255.7 %all-reduce.14.cloned.1.call-start = ((), (), s32[]{:S(2)}) async-start(), calls=%async_computation | async-start | bytes 2654208 | tf_op jit(solution)/shard_map/psum | solution.py:167
  11.0 1.4 copy-start.1
  11.8 16.4 %copy-start.2 = (bf16[3,96,3,3,96]{4,1,0,3,2:T(8,128)(2,1)}, bf16[3,96,3,3,96]{4,1,0,3,2:T(8,128)(2,1)S(1)}, u32[]{:S(2)}) copy-start(bf16[3,96,3,3,96]{4,1,0,3,2:T(8,128)(2,1)S(1)} %copy.339) | copy-start | bytes 1492996
  14.1 46.2 %collective-permute-start.9 = (f32[96,1,128]{2,0,1:T(8,128)}, f32[96,1,128]{2,0,1:T(8,128)}, u32[]{:S(2)}, u32[]{:S(2)}) collective-permute-start(f32[96,1,128]{2,0,1:T(8,128)} %slice.759), channel_id=1, source_target_pairs={} | collective-permute-start | bytes 147464 | tf_op jit(solution)/shard_map/ppermute | solution.py:14
  15.7 3.7 %copy-start.11 = (bf16[2,2,2,96,8,128]{5,3,2,4,1,0:T(8,128)(2,1)}, bf16[2,2,2,96,8,128]{5,3,2,4,1,0:T(8,128)(2,1)S(1)}, u32[]{:S(2)}) copy-start(bf16[2,2,2,96,8,128]{5,3,2,4,1,0:T(8,128)(2,1)S(1)} %copy.174) | copy-start | bytes 4718596
  16.0 1.0 copy-start.15
  17.6 48.1 %collective-permute-start.7 = (f32[96,1,128]{2,0,1:T(8,128)}, f32[96,1,128]{2,0,1:T(8,128)S(1)}, u32[]{:S(2)}, u32[]{:S(2)}) collective-permute-start(f32[96,1,128]{2,0,1:T(8,128)} %slice.753), channel_id=1, source_target_pairs={} | collective-permute-start | bytes 147464 | tf_op jit(solution)/shard_map/ppermute | solution.py:14
  19.5 38.9 %collective-permute-start.2 = (f32[96,8,16]{2,0,1:T(8,128)}, f32[96,8,16]{2,0,1:T(8,128)}, u32[]{:S(2)}, u32[]{:S(2)}) collective-permute-start(f32[96,8,16]{2,0,1:T(8,128)} %slice.738), channel_id=1, source_target_pairs={{0,8},{4,12},{8,16},{12,20},{16,24},{20,28},{1,9},{5,13},{9,17},{1... | collective-permute-start | bytes 147464 | tf_op jit(solution)/shard_map/ppermute | solution.py:14
  26.2 4.9 %copy-start.16 = (f32[96,8,128]{2,0,1:T(8,128)}, f32[96,8,128]{2,0,1:T(8,128)S(1)}, u32[]{:S(2)}) copy-start(f32[96,8,128]{2,0,1:T(8,128)S(1)} %convolution_bitcast_fusion.6) | copy-start | bytes 1179652
  26.9 44.3 %collective-permute-start.5 = (f32[96,1,128]{2,0,1:T(8,128)}, f32[96,1,128]{2,0,1:T(8,128)}, u32[]{:S(2)}, u32[]{:S(2)}) collective-permute-start(f32[96,1,128]{2,0,1:T(8,128)} %slice.747), channel_id=1, source_target_pairs={} | collective-permute-start | bytes 147464 | tf_op jit(solution)/shard_map/ppermute | solution.py:14
  28.5 4.8 %copy-start.17 = (f32[96,8,128]{2,0,1:T(8,128)}, f32[96,8,128]{2,0,1:T(8,128)S(1)}, u32[]{:S(2)}) copy-start(f32[96,8,128]{2,0,1:T(8,128)S(1)} %convolution_bitcast_fusion.14) | copy-start | bytes 1179652
  31.1 17.1 %collective-permute-start = (f32[96,8,8]{2,0,1:T(8,128)}, f32[96,8,8]{2,0,1:T(8,128)}, u32[]{:S(2)}, u32[]{:S(2)}) collective-permute-start(f32[96,8,8]{2,0,1:T(8,128)} %slice.639), channel_id=1, source_target_pairs={{0,4},{4,8},{8,12},{12,16},{16,20},{20,24},{24,28},{1,5},{5,9},{9,... | collective-permute-start | bytes 73736 | tf_op jit(solution)/shard_map/ppermute | solution.py:14
  33.4 1.3 copy-start.3
  34.4 0.9 copy-start.6
  34.4 2.6 copy-start.26
  34.4 3.2 %copy-start.27 = (s32[4]{0:T(128)S(1)}, s32[4]{0:T(128)}, u32[]{:S(2)}) copy-start(s32[4]{0:T(128)} %constant.474.clone.1) | copy-start | bytes 52
  45.5 1.7 copy-start.7
  48.2 29.1 %collective-permute-start.1 = (f32[96,8,16]{2,0,1:T(8,128)}, f32[96,8,16]{2,0,1:T(8,128)}, u32[]{:S(2)}, u32[]{:S(2)}) collective-permute-start(f32[96,8,16]{2,0,1:T(8,128)} %slice.734), channel_id=1, source_target_pairs={{0,8},{4,12},{8,16},{12,20},{16,24},{20,28},{1,9},{5,13},{9,17},{1... | collective-permute-start | bytes 147464 | tf_op jit(solution)/shard_map/ppermute | solution.py:14
  58.3 2.0 copy-start.8
  58.3 21.0 %collective-permute-start.4 = (f32[96,1,128]{2,0,1:T(8,128)}, f32[96,1,128]{2,0,1:T(8,128)S(1)}, u32[]{:S(2)}, u32[]{:S(2)}) collective-permute-start(f32[96,1,128]{2,0,1:T(8,128)} %slice.743), channel_id=1, source_target_pairs={} | collective-permute-start | bytes 147464 | tf_op jit(solution)/shard_map/ppermute | solution.py:14
  59.2 6.5 %copy-start.10 = (f32[96,7,128]{2,0,1:T(8,128)S(1)}, f32[96,7,128]{2,0,1:T(8,128)}, u32[]{:S(2)}) copy-start(f32[96,7,128]{2,0,1:T(8,128)} %slice.754) | copy-start | bytes 1032196
  60.3 14.4 %copy-start.9 = (f32[96,7,128]{2,0,1:T(8,128)S(1)}, f32[96,7,128]{2,0,1:T(8,128)}, u32[]{:S(2)}) copy-start(f32[96,7,128]{2,0,1:T(8,128)} %slice.748) | copy-start | bytes 1032196
  61.3 21.2 %collective-permute-start.10 = (f32[96,8,16]{2,0,1:T(8,128)}, f32[96,8,16]{2,0,1:T(8,128)}, u32[]{:S(2)}, u32[]{:S(2)}) collective-permute-start(f32[96,8,16]{2,0,1:T(8,128)} %slice_maximum_fusion), channel_id=1, source_target_pairs={{0,8},{4,12},{8,16},{12,20},{16,24},{20,28},{1,9},{5,13},{9,17},{1... | collective-permute-start | bytes 147464 | tf_op jit(solution)/shard_map/ppermute | solution.py:14
  66.6 32.7 %collective-permute-start.8 = (f32[96,8,16]{2,0,1:T(8,128)}, f32[96,8,16]{2,0,1:T(8,128)}, u32[]{:S(2)}, u32[]{:S(2)}) collective-permute-start(f32[96,8,16]{2,0,1:T(8,128)} %slice_maximum_fusion.1), channel_id=1, source_target_pairs={{0,8},{4,12},{8,16},{12,20},{16,24},{20,28},{1,9},{5,13},{9,17},{1... | collective-permute-start | bytes 147464 | tf_op jit(solution)/shard_map/ppermute | solution.py:14
  71.2 9.0 %collective-permute-start.3 = (f32[96,8,8]{2,0,1:T(8,128)}, f32[96,8,8]{2,0,1:T(8,128)}, u32[]{:S(2)}, u32[]{:S(2)}) collective-permute-start(f32[96,8,8]{2,0,1:T(8,128)} %slice.649), channel_id=1, source_target_pairs={{0,4},{4,8},{8,12},{12,16},{16,20},{20,24},{24,28},{1,5},{5,9},{9,... | collective-permute-start | bytes 73736 | tf_op jit(solution)/shard_map/ppermute | solution.py:14
  77.3 2.9 %collective-permute-start.6 = (f32[96,8,8]{2,0,1:T(8,128)}, f32[96,8,8]{2,0,1:T(8,128)S(1)}, u32[]{:S(2)}, u32[]{:S(2)}) collective-permute-start(f32[96,8,8]{2,0,1:T(8,128)} %slice.659), channel_id=1, source_target_pairs={{0,4},{4,8},{8,12},{12,16},{16,20},{20,24},{24,28},{1,5},{5,9},{9,... | collective-permute-start | bytes 73736 | tf_op jit(solution)/shard_map/ppermute | solution.py:14
  84.7 17.1 %slice-start = ((f32[96,8,128]{2,0,1:T(8,128)}), f32[96,7,128]{2,0,1:T(8,128)S(1)}, s32[]{:S(2)}) async-start(f32[96,8,128]{2,0,1:T(8,128)} %convolution_bitcast_fusion.12), calls=%async_computation.1 | async-start | bytes 688128 | tf_op jit(solution)/shard_map/slice | solution.py:22
  84.7 17.0 %copy-start.25 = (pred[128]{0:T(512)(128)(4,1)S(1)}, pred[128]{0:T(512)(128)(4,1)}, u32[]{:S(2)}) copy-start(pred[128]{0:T(512)(128)(4,1)} %compare_and_fusion) | copy-start | bytes 388
  84.7 15.9 %collective-permute-start.11 = (f32[96,8,8]{2,0,1:T(8,128)S(1)}, f32[96,8,8]{2,0,1:T(8,128)S(1)}, u32[]{:S(2)}, u32[]{:S(2)}) collective-permute-start(f32[96,8,8]{2,0,1:T(8,128)S(1)} %slice.673), channel_id=1, source_target_pairs={{0,4},{4,8},{8,12},{12,16},{16,20},{20,24},{24,28},{1,5},{5,9},{9,... | collective-permute-start | bytes 73736 | tf_op jit(solution)/shard_map/ppermute | solution.py:14
  101.8 2.5 copy-start.28
  101.8 3.0 %copy-start.22 = (bf16[1,96,8,128]{3,2,1,0:T(8,128)(2,1)S(1)}, bf16[1,96,8,128]{3,2,1,0:T(8,128)(2,1)}, u32[]{:S(2)}) copy-start(bf16[1,96,8,128]{3,2,1,0:T(8,128)(2,1)} %param.35) | copy-start | bytes 589828
  136.9 5.7 %collective-permute-start.12 = (bf16[96,8,8]{2,0,1:T(8,128)(2,1)}, bf16[96,8,8]{2,0,1:T(8,128)(2,1)S(1)}, u32[]{:S(2)}, u32[]{:S(2)}) collective-permute-start(bf16[96,8,8]{2,0,1:T(8,128)(2,1)} %slice.676), channel_id=1, source_target_pairs={{4,0},{8,4},{12,8},{16,12},{20,16},{24,20},{28,24},{5,1},{9,5},{13... | collective-permute-start | bytes 36872 | tf_op jit(solution)/shard_map/ppermute | solution.py:14
  138.9 16.1 %copy-start.13 = (bf16[96,8,112]{2,0,1:T(8,128)(2,1)}, bf16[96,8,112]{2,0,1:T(8,128)(2,1)S(1)}, u32[]{:S(2)}) copy-start(bf16[96,8,112]{2,0,1:T(8,128)(2,1)S(1)} %slice.766) | copy-start | bytes 516100
  139.7 6.6 %collective-permute-start.15 = (bf16[96,1,128]{2,0,1:T(8,128)(2,1)S(1)}, bf16[96,1,128]{2,0,1:T(8,128)(2,1)S(1)}, u32[]{:S(2)}, u32[]{:S(2)}) collective-permute-start(bf16[96,1,128]{2,0,1:T(8,128)(2,1)S(1)} %slice.771), channel_id=1, source_target_pairs={} | collective-permute-start | bytes 73736 | tf_op jit(solution)/shard_map/ppermute | solution.py:14
  140.3 13.6 %collective-permute-start.13 = (bf16[96,8,16]{2,0,1:T(8,128)(2,1)S(1)}, bf16[96,8,16]{2,0,1:T(8,128)(2,1)}, u32[]{:S(2)}, u32[]{:S(2)}) collective-permute-start(bf16[96,8,16]{2,0,1:T(8,128)(2,1)S(1)} %bitcast.549), channel_id=1, source_target_pairs={{8,0},{12,4},{16,8},{20,12},{24,16},{28,20},{9,1},{13,5},{17,9},{2... | collective-permute-start | bytes 73736 | tf_op jit(solution)/shard_map/ppermute | solution.py:14
  148.6 25.0 %collective-permute-start.17 = (bf16[96,8,16]{2,0,1:T(8,128)(2,1)}, bf16[96,8,16]{2,0,1:T(8,128)(2,1)}, u32[]{:S(2)}, u32[]{:S(2)}) collective-permute-start(bf16[96,8,16]{2,0,1:T(8,128)(2,1)} %fusion.70), channel_id=1, source_target_pairs={{8,0},{12,4},{16,8},{20,12},{24,16},{28,20},{9,1},{13,5},{17,9},{2... | collective-permute-start | bytes 73736 | tf_op jit(solution)/shard_map/ppermute | solution.py:14
  152.7 7.3 %collective-permute-start.16 = (bf16[96,8,8]{2,0,1:T(8,128)(2,1)}, bf16[96,8,8]{2,0,1:T(8,128)(2,1)}, u32[]{:S(2)}, u32[]{:S(2)}) collective-permute-start(bf16[96,8,8]{2,0,1:T(8,128)(2,1)} %slice.684), channel_id=1, source_target_pairs={{4,0},{8,4},{12,8},{16,12},{20,16},{24,20},{28,24},{5,1},{9,5},{13... | collective-permute-start | bytes 36872 | tf_op jit(solution)/shard_map/ppermute | solution.py:14
  158.7 6.5 %collective-permute-start.14 = (bf16[96,8,8]{2,0,1:T(8,128)(2,1)}, bf16[96,8,8]{2,0,1:T(8,128)(2,1)}, u32[]{:S(2)}, u32[]{:S(2)}) collective-permute-start(bf16[96,8,8]{2,0,1:T(8,128)(2,1)} %slice.680), channel_id=1, source_target_pairs={{4,0},{8,4},{12,8},{16,12},{20,16},{24,20},{28,24},{5,1},{9,5},{13... | collective-permute-start | bytes 36872 | tf_op jit(solution)/shard_map/ppermute | solution.py:14
  170.3 2.3 copy-start.19
  176.5 5.2 %collective-permute-start.18 = (bf16[96,8,8]{2,0,1:T(8,128)(2,1)}, bf16[96,8,8]{2,0,1:T(8,128)(2,1)S(1)}, u32[]{:S(2)}, u32[]{:S(2)}) collective-permute-start(bf16[96,8,8]{2,0,1:T(8,128)(2,1)} %slice.688), channel_id=1, source_target_pairs={{4,0},{8,4},{12,8},{16,12},{20,16},{24,20},{28,24},{5,1},{9,5},{13... | collective-permute-start | bytes 36872 | tf_op jit(solution)/shard_map/ppermute | solution.py:14
  183.1 4.1 %copy-start.4 = (bf16[4,96,8,128]{3,1,2,0:T(8,128)(2,1)S(1)}, bf16[4,96,8,128]{3,1,2,0:T(8,128)(2,1)}, u32[]{:S(2)}) copy-start(bf16[4,96,8,128]{3,1,2,0:T(8,128)(2,1)} %copy.215) | copy-start | bytes 2359300
  187.7 2.4 copy-start.12
  187.7 2.6 copy-start.21
  190.5 2.7 copy-start.18
  190.6 4.8 %copy-start.23 = (bf16[1,1,2,96,8,128]{5,4,3,2,1,0:T(8,128)(2,1)S(1)}, bf16[1,1,2,96,8,128]{5,4,3,2,1,0:T(8,128)(2,1)}, u32[]{:S(2)}) copy-start(bf16[1,1,2,96,8,128]{5,4,3,2,1,0:T(8,128)(2,1)} %slice.796) | copy-start | bytes 1179652
  192.8 2.9 %copy-start.24 = (bf16[1,1,1,96,8,128]{5,4,3,2,1,0:T(8,128)(2,1)S(1)}, bf16[1,1,1,96,8,128]{5,4,3,2,1,0:T(8,128)(2,1)}, u32[]{:S(2)}) copy-start(bf16[1,1,1,96,8,128]{5,4,3,2,1,0:T(8,128)(2,1)} %get-tuple-element.179) | copy-start | bytes 589828
  197.1 1.9 copy-start.5
  (2 other events, 1.7 us)
Sparse Core Ops, SparseCore 0:
  197.2 65.5 all-reduce.13
where the time goes:
time: 280 us; the launch traced here: 278 us
  local copies, waits for them, and re-layouts  68.1 us (24%)
  waiting for transfers between devices  59.4 us (21%)
  starting transfers between devices  49.2 us (18%)
  other arithmetic  31.8 us (11%)
  blocking collectives  28.4 us (10%)
  matrix products  25.8 us (9%)
  between operations  14.9 us (5%)
    psum x1, waiting for transfers between devices, shards(): lax.psum((local_kernel, gamma_local, beta_local), 'space')  55.8 us
    ppermute x19, starting transfers between devices, from_behind(): lax.ppermute(value, axis, [(source, source + steps) for source in range(l...  49.2 us
    psum x1, blocking collectives, shards(): lax.psum((local_kernel, gamma_local, beta_local), 'space')  28.4 us
    dot_general x12, matrix products, kernel_plane(): jnp.einsum('oxl,bcixl->obci', shifted_grad[shift_x, shift_y, shift_z], st...  11.5 us
    slice x4, local copies, waits for them, and re-layouts, pull_lower(): sliver = field[..., span_z - 1::span_z]  9.58 us
    unnamed x62, local copies, waits for them, and re-layouts  9.1 us
    slice x4, local copies, waits for them, and re-layouts, pull_upper(): sliver = field[..., 0::span_z]  8.13 us
    dot_general x8, matrix products, shards(): jnp.einsum('oabci,abcoxl->ixl', weights_sel, grad_sel, preferred_element_...  7.73 us
  transfers between devices with their start and end apart: 20, of which 3 were waited for; matrix products, arithmetic and copies ran while one was open for 30% of the time, Pallas kernels for 0%

commit v1 on v0

v1 whole, which is shorter than its diff:
```python
import functools
import math

import jax
import jax.numpy as jnp
from jax import lax
from jax.experimental import pallas as pl
from jax.experimental.pallas import tpu as pltpu
from jax.sharding import PartitionSpec as P

BF = jnp.bfloat16
F32 = jnp.float32
C = 96
NX = 8
LANES = 128
SZ = 16
ROWS = 9 * C
MESH = pl.DeviceIdType.MESH


def taps_of(parity):
    return ((1, 0),) if parity == 0 else ((2, 0), (0, 1))


def row_of(ty, tz):
    return (ty * 3 + tz) * C


def tile(x):
    return pl.ds(x * LANES, LANES)


def body(groups, scale, vol, ker, beta, gamma, cot, norm_o, dvol_o, kg_o, gg_o, bg_o,
         tmp, V, Yp, Zp, Yr, Zr, Cr, Kf, WB, Gs, up, S, GY, GZ, GYr, GZr, GCr,
         part, sendA, recvA, sendB, recvB, full, gacc, bacc,
         ysend, yrecv, zsend, zrecv, csend, crecv, xsend, xrecv,
         asend, arecv, bsend, brecv, gsend, grecv, dsend, drecv):
    idx = lax.axis_index("space")
    gx = idx // 8
    by = idx // 2 % 4
    bz = idx % 2
    base = gx * 8

    def dev(jy, jz):
        return {"space": base + jy * 2 + jz}

    barrier = pltpu.get_barrier_semaphore()
    for k in range(1, 8):
        peer = base + (idx - base + k) % 8
        pl.semaphore_signal(barrier, inc=1, device_id={"space": peer}, device_id_type=MESH)
    if groups > 1:
        @pl.when(gx > 0)
        def _():
            pl.semaphore_signal(barrier, inc=1, device_id={"space": idx - 8}, device_id_type=MESH)

        @pl.when(gx < groups - 1)
        def _():
            pl.semaphore_signal(barrier, inc=1, device_id={"space": idx + 8}, device_id_type=MESH)

    lane = lax.broadcasted_iota(jnp.int32, (C, LANES), 1)
    lz = lane % SZ
    ly = lane // SZ

    def roll(value, shift):
        shift = shift % LANES
        return value if shift == 0 else pltpu.roll(value, shift, 1)

    def remote(src, dst, ss, rs, target):
        return pltpu.make_async_remote_copy(
            src_ref=src, dst_ref=dst, send_sem=ss, recv_sem=rs,
            device_id=target, device_id_type=MESH)

    def spread_in(px, _):
        for py, pz in ((1, 1), (1, 0), (0, 1), (0, 0)):
            r = row_of(1 + py, 1 + pz)
            tmp[...] = vol[px * 4 + py * 2 + pz].astype(F32).reshape(C * NX, LANES)
            ya = jnp.zeros((C, LANES), F32)
            za = jnp.zeros((C, LANES), F32)
            for x in range(NX):
                t = tmp[pl.ds(x, C, stride=NX), :]
                V[px, r:r + C, tile(x + 1)] = t.astype(BF)
                if py:
                    ya = jnp.where(ly == x, roll(t, x * SZ - 112), ya)
                if pz:
                    za = jnp.where(lz == x, roll(t, x - 15), za)
            if py:
                Yp[px, pz] = ya.astype(BF)
            if pz:
                Zp[px, py] = za.astype(BF)
        return 0

    lax.fori_loop(0, 2, spread_in, 0)

    pl.semaphore_wait(barrier, 7)
    if groups > 1:
        @pl.when(gx > 0)
        def _():
            pl.semaphore_wait(barrier, 1)

        @pl.when(gx < groups - 1)
        def _():
            pl.semaphore_wait(barrier, 1)

    y_copy = remote(Yp, Yr, ysend, yrecv, dev((by + 1) % 4, bz))
    z_copy = remote(Zp, Zr, zsend, zrecv, dev(by, 1 - bz))
    c_copy = [remote(Yp.at[px, 1], Cr.at[px], csend.at[px], crecv.at[px], dev((by + 1) % 4, 1 - bz))
              for px in range(2)]

    @pl.when(by < 3)
    def _():
        y_copy.start()

        @pl.when(bz == 0)
        def _():
            for c in c_copy:
                c.start()

    @pl.when(bz == 0)
    def _():
        z_copy.start()

    for tx in range(3):
        Kf[tx] = ker[:, tx * ROWS:(tx + 1) * ROWS]
    WB[...] = jnp.zeros_like(WB)
    for tx in range(3):
        for py in range(2):
            for pz in range(2):
                q = (py * 2 + pz) * C
                for ty, sy in taps_of(py):
                    for tz, sz in taps_of(pz):
                        t = tx * 9 + ty * 3 + tz
                        w = ker[:, t * C:(t + 1) * C].astype(F32)
                        v = (sy * 2 + sz) * LANES
                        WB[tx, q:q + C, v:v + C] = w.T.astype(BF)
    for v in range(4):
        Gs[v * LANES + C:(v + 1) * LANES, :] = jnp.zeros((LANES - C, 9 * LANES), BF)
    if groups == 1:
        Gs[:, 8 * LANES:] = jnp.zeros((4 * LANES, LANES), BF)
        V[1, :, 0:LANES] = jnp.zeros((ROWS, LANES), BF)
    tmp[...] = cot[0].astype(F32).reshape(C * NX, LANES)
    for x in range(NX):
        up[:, tile(x)] = tmp[pl.ds(x, C, stride=NX), :]
    gam = gamma[...]
    gam_b = gam.astype(BF)
    gam_t = gam.T.astype(BF)
    eye = (lax.broadcasted_iota(jnp.int32, (C, C), 0) == lax.broadcasted_iota(jnp.int32, (C, C), 1))
    beta_col = jnp.sum(jnp.where(eye, beta[...], 0.0), axis=1, keepdims=True)

    @pl.when(by > 0)
    def _():
        y_copy.wait_recv()

        @pl.when(bz == 1)
        def _():
            for c in c_copy:
                c.wait_recv()

    @pl.when(by == 0)
    def _():
        Yr[...] = jnp.zeros_like(Yr)

    @pl.when((by == 0) | (bz == 0))
    def _():
        Cr[...] = jnp.zeros_like(Cr)

    @pl.when(bz == 1)
    def _():
        z_copy.wait_recv()

    @pl.when(bz == 0)
    def _():
        Zr[...] = jnp.zeros_like(Zr)

    def shifted(px, _):
        y0 = Yr[px, 0].astype(F32)
        y1 = Yr[px, 1].astype(F32)
        z0 = Zr[px, 0].astype(F32)
        z1 = Zr[px, 1].astype(F32)
        yz = jnp.where(lz == 0, roll(Cr[px].astype(F32), -15), roll(y1, 1))
        for x in range(NX):
            def get(ty, tz):
                r = row_of(ty, tz)
                return V[px, r:r + C, tile(x + 1)].astype(F32)

            def put(ty, tz, value):
                r = row_of(ty, tz)
                V[px, r:r + C, tile(x + 1)] = value.astype(BF)

            put(1, 0, jnp.where(lz == 0, roll(z0, -x), roll(get(1, 2), 1)))
            put(0, 1, jnp.where(ly == 0, roll(y0, -SZ * x), roll(get(2, 1), SZ)))
            d = get(2, 2)
            t = jnp.where(lz == 0, roll(z1, -x), roll(d, 1))
            put(2, 0, t)
            put(0, 2, jnp.where(ly == 0, roll(y1, -SZ * x), roll(d, SZ)))
            put(0, 0, jnp.where(ly == 0, roll(yz, -SZ * x), roll(t, SZ)))
        return 0

    lax.fori_loop(0, 2, shifted, 0)

    if groups > 1:
        x_copy = remote(V.at[1, :, pl.ds(8 * LANES, LANES)], V.at[1, :, pl.ds(0, LANES)],
                        xsend.at[0], xrecv.at[0], {"space": (idx + 8) % (groups * 8)})

        @pl.when(gx < groups - 1)
        def _():
            x_copy.start()

        @pl.when(gx > 0)
        def _():
            x_copy.wait_recv()

        @pl.when(gx == 0)
        def _():
            V[1, :, 0:LANES] = jnp.zeros((ROWS, LANES), BF)

    gacc[...] = jnp.zeros_like(gacc)
    bacc[...] = jnp.zeros_like(bacc)

    def forward(i, _):
        lo = pl.multiple_of(i * 256, 256)
        hi = pl.multiple_of(i * 256 + LANES, LANES)
        conv = jnp.dot(Kf[1], V[0, :, pl.ds(hi, 256)], preferred_element_type=F32)
        conv += jnp.dot(Kf[0], V[1, :, pl.ds(lo, 256)], preferred_element_type=F32)
        conv += jnp.dot(Kf[2], V[1, :, pl.ds(hi, 256)], preferred_element_type=F32)
        sq = conv * conv
        sq_b = sq.astype(BF)
        r = lax.rsqrt(beta_col + jnp.dot(gam_b, sq_b, preferred_element_type=F32))
        u = up[:, pl.ds(lo, 256)]
        normalized = conv * r
        weighted = -0.5 * u * conv * r * r * r
        w_b = weighted.astype(BF)
        coupled = jnp.dot(gam_t, w_b, preferred_element_type=F32)
        g = u * r + 2.0 * conv * coupled
        Gs[0:C, pl.ds(lo, 256)] = g.astype(BF)
        gacc[...] += lax.dot_general(w_b, sq_b, (((1,), (1,)), ((), ())), preferred_element_type=F32)
        bacc[...] += weighted[:, :LANES] + weighted[:, LANES:]
        for xx in range(2):
            tmp[pl.ds(i * 2 + xx, C, stride=NX), :] = normalized[:, xx * LANES:(xx + 1) * LANES]
        return 0

    lax.fori_loop(0, 4, forward, 0)
    norm_o[0] = tmp[...].reshape(C, NX, LANES).astype(BF)

    ya = jnp.zeros((C, LANES), F32)
    za = jnp.zeros((C, LANES), F32)
    for x in range(NX):
        t = Gs[0:C, tile(x)].astype(F32)
        ya = jnp.where(ly == x, roll(t, x * SZ), ya)
        za = jnp.where(lz == x, roll(t, x), za)
    GY[...] = ya.astype(BF)
    GZ[...] = za.astype(BF)
    gy_copy = remote(GY, GYr, gsend.at[0], grecv.at[0], dev((by + 3) % 4, bz))
    gz_copy = remote(GZ, GZr, gsend.at[1], grecv.at[1], dev(by, 1 - bz))
    gc_copy = remote(GY, GCr, gsend.at[2], grecv.at[2], dev((by + 3) % 4, 1 - bz))

    @pl.when(by > 0)
    def _():
        gy_copy.start()

        @pl.when(bz == 1)
        def _():
            gc_copy.start()

    @pl.when(bz == 1)
    def _():
        gz_copy.start()

    nt = (((1,), (1,)), ((), ()))
    for tx in range(3):
        first = 0 if tx == 0 else LANES
        plane = 0 if tx == 1 else 1
        for s in range(4):
            n = min(256, ROWS - s * 256)
            k = lax.dot_general(Gs[0:C, 0:8 * LANES],
                                V[plane, s * 256:s * 256 + n, first:first + 8 * LANES],
                                nt, preferred_element_type=F32) * scale
            if n == 256:
                part[tx * 7 + s * 2] = k[:, :LANES]
                part[tx * 7 + s * 2 + 1] = k[:, LANES:]
            else:
                part[tx * 7 + s * 2] = jnp.concatenate([k, jnp.zeros((C, LANES - C), F32)], axis=1)
    bsum = jnp.sum(bacc[...], axis=1, keepdims=True) * scale
    part[21] = jnp.concatenate(
        [gacc[...] * scale, jnp.broadcast_to(bsum, (C, LANES - C))], axis=1)
    part[22] = jnp.zeros((C, LANES), F32)
    part[23] = jnp.zeros((C, LANES), F32)

    def to_a(i, _):
        sendA[i] = part[(1 - bz) * 12 + i].astype(BF)
        return 0

    lax.fori_loop(0, 12, to_a, 0)
    a_copy = remote(sendA, recvA, asend, arecv, dev(by, 1 - bz))
    a_copy.start()

    @pl.when(by < 3)
    def _():
        gy_copy.wait_recv()

        @pl.when(bz == 0)
        def _():
            gc_copy.wait_recv()

    @pl.when(bz == 0)
    def _():
        gz_copy.wait_recv()

    @pl.when(by == 3)
    def _():
        GYr[...] = jnp.zeros_like(GYr)

    @pl.when((by == 3) | (bz == 1))
    def _():
        GCr[...] = jnp.zeros_like(GCr)

    @pl.when(bz == 1)
    def _():
        GZr[...] = jnp.zeros_like(GZr)

    y = GYr[...].astype(F32)
    z = GZr[...].astype(F32)
    yz = jnp.where(lz == SZ - 1, roll(GCr[...].astype(F32), 15), roll(y, -1))
    for x in range(NX):
        g = Gs[0:C, tile(x)].astype(F32)
        t = jnp.where(lz == SZ - 1, roll(z, 15 - x), roll(g, -1))
        Gs[LANES:LANES + C, tile(x)] = t.astype(BF)
        Gs[2 * LANES:2 * LANES + C, tile(x)] = jnp.where(
            ly == 7, roll(y, 112 - SZ * x), roll(g, -SZ)).astype(BF)
        Gs[3 * LANES:3 * LANES + C, tile(x)] = jnp.where(
            ly == 7, roll(yz, 112 - SZ * x), roll(t, -SZ)).astype(BF)

    if groups > 1:
        h_copy = remote(Gs.at[:, pl.ds(0, LANES)], Gs.at[:, pl.ds(8 * LANES, LANES)],
                        xsend.at[1], xrecv.at[1], {"space": (idx + (groups - 1) * 8) % (groups * 8)})

        @pl.when(gx > 0)
        def _():
            h_copy.start()

        @pl.when(gx < groups - 1)
        def _():
            h_copy.wait_recv()

        @pl.when(gx == groups - 1)
        def _():
            Gs[:, 8 * LANES:] = jnp.zeros((4 * LANES, LANES), BF)

    a_copy.wait()

    def add_a(i, _):
        j = bz * 12 + i
        total = part[j] + recvA[i].astype(F32)
        part[j] = total
        sendB[i // 3, i % 3] = total.astype(BF)
        return 0

    lax.fori_loop(0, 12, add_a, 0)
    b_copy = []
    for k in range(1, 4):
        to = (by + k) % 4
        b_copy.append(remote(sendB.at[to], recvB.at[k], bsend.at[k], brecv.at[k], dev(to, bz)))
        b_copy[-1].start()

    def back(px):
        def step(i, _):
            lo = pl.multiple_of(i * 256, 256)
            hi = pl.multiple_of(i * 256 + LANES, LANES)
            if px == 0:
                res = jnp.dot(WB[1], Gs[:, pl.ds(lo, 256)], preferred_element_type=F32)
            else:
                res = jnp.dot(WB[2], Gs[:, pl.ds(lo, 256)], preferred_element_type=F32)
                res += jnp.dot(WB[0], Gs[:, pl.ds(hi, 256)], preferred_element_type=F32)
            for q in range(4):
                for xx in range(2):
                    S[pl.ds(q * C * NX + i * 2 + xx, C, stride=NX), :] = (
                        res[q * C:(q + 1) * C, xx * LANES:(xx + 1) * LANES])
            return 0

        lax.fori_loop(0, 4, step, 0)
        for q in range(4):
            dvol_o[px * 4 + q] = S[q * C * NX:(q + 1) * C * NX].reshape(C, NX, LANES).astype(BF)

    back(0)

    for c in b_copy:
        c.wait()
    for i in range(3):
        total = part[bz * 12 + by * 3 + i]
        for k in range(1, 4):
            total += recvB[k, i].astype(F32)
        full[bz, by, i] = total.astype(BF)
    d_copy = []
    for k in range(1, 4):
        to = (by + k) % 4
        d_copy.append(remote(full.at[bz, by], full.at[bz, by], dsend.at[k], drecv.at[k], dev(to, bz)))
        d_copy[-1].start()

    back(1)

    for k in range(1, 4):
        source = (by + 4 - k) % 4
        remote(full.at[bz, source], full.at[bz, source], dsend.at[k], drecv.at[k],
               dev((by + k) % 4, bz)).wait()
    e_copy = remote(full.at[bz], full.at[bz], dsend.at[0], drecv.at[0], dev(by, 1 - bz))
    e_copy.start()
    e_copy.wait_send()
    remote(full.at[1 - bz], full.at[1 - bz], dsend.at[0], drecv.at[0], dev(by, 1 - bz)).wait_recv()

    for tx in range(3):
        for s in range(7):
            j = tx * 7 + s
            n = min(LANES, ROWS - s * LANES)
            at = tx * ROWS + s * LANES
            kg_o[:, at:at + n] = full[j // 12, j % 12 // 3, j % 3][:, :n].astype(F32)
    last = full[1, 3, 0].astype(F32)
    gg_o[...] = last[:, :C]
    bg_o[...] = jnp.sum(jnp.where(eye, last[:, C:C + 1], 0.0), axis=0, keepdims=True)

    @pl.when(by < 3)
    def _():
        y_copy.wait_send()

        @pl.when(bz == 0)
        def _():
            for c in c_copy:
                c.wait_send()

    @pl.when(bz == 0)
    def _():
        z_copy.wait_send()

    @pl.when(by > 0)
    def _():
        gy_copy.wait_send()

        @pl.when(bz == 1)
        def _():
            gc_copy.wait_send()

    @pl.when(bz == 1)
    def _():
        gz_copy.wait_send()

    if groups > 1:
        @pl.when(gx < groups - 1)
        def _():
            x_copy.wait_send()

        @pl.when(gx > 0)
        def _():
            h_copy.wait_send()


def shards(volume, kernel, beta, gamma, cotangent):
    devices = lax.axis_size("space")
    groups = devices // 8
    scale = 1.0 / math.sqrt(NX * LANES * devices)
    vm = lambda *shape, dtype=BF: pltpu.VMEM(shape, dtype)
    dma = lambda *shape: pltpu.SemaphoreType.DMA(shape) if shape else pltpu.SemaphoreType.DMA
    spec = pl.BlockSpec(memory_space=pltpu.VMEM)
    out = pl.pallas_call(
        functools.partial(body, groups, scale),
        out_shape=(
            jax.ShapeDtypeStruct((1, C, NX, LANES), BF),
            jax.ShapeDtypeStruct((8, C, NX, LANES), BF),
            jax.ShapeDtypeStruct((C, 27 * C), F32),
            jax.ShapeDtypeStruct((C, C), F32),
            jax.ShapeDtypeStruct((1, C), F32),
        ),
        in_specs=[spec] * 5,
        out_specs=(spec,) * 5,
        scratch_shapes=[
            vm(C * NX, LANES, dtype=F32), vm(2, ROWS, 9 * LANES),
            vm(2, 2, C, LANES), vm(2, 2, C, LANES), vm(2, 2, C, LANES), vm(2, 2, C, LANES), vm(2, C, LANES),
            vm(3, C, ROWS), vm(3, 4 * C, 4 * LANES), vm(4 * LANES, 9 * LANES),
            vm(C, NX * LANES, dtype=F32), vm(4 * C * NX, LANES, dtype=F32),
            vm(C, LANES), vm(C, LANES), vm(C, LANES), vm(C, LANES), vm(C, LANES),
            vm(24, C, LANES, dtype=F32), vm(12, C, LANES), vm(12, C, LANES),
            vm(4, 3, C, LANES), vm(4, 3, C, LANES), vm(2, 4, 3, C, LANES),
            vm(C, C, dtype=F32), vm(C, LANES, dtype=F32),
            dma(), dma(), dma(), dma(), dma(2), dma(2), dma(2), dma(2),
            dma(), dma(), dma(4), dma(4), dma(3), dma(3), dma(4), dma(4),
        ],
        compiler_params=pltpu.CompilerParams(
            collective_id=0, has_side_effects=True, vmem_limit_bytes=48 * 1024 * 1024),
    )(volume, kernel, beta.reshape(1, C), gamma, cotangent)
    normalized, dvol, kg, gg, bg = out
    if groups > 1:
        kg, gg, bg = jax.tree.map(lambda a: a * 0.125, lax.psum((kg, gg, bg), "space"))
    return normalized, dvol, kg, gg, bg.reshape(C)


def solution(mesh):
    blocks = P(("dp", "space"), None, None, None)
    return jax.shard_map(
        shards,
        mesh=mesh,
        in_specs=(blocks, P(), P(), P(), blocks),
        out_specs=(blocks, blocks, P("dp", None), P("dp", None), P("dp")),
        check_vma=False,
    )
```

time: 280 us -> 37.9 us (0.14)
  waiting for transfers between devices: 59.4 us -> 0 us
  local copies, waits for them, and re-layouts: 68.1 us -> 8.73 us
  starting transfers between devices: 49.2 us -> 0 us
  other arithmetic: 31.8 us -> 0 us
  blocking collectives: 28.4 us -> 0 us
  Pallas kernels: 0 us -> 28.2 us
  matrix products: 25.8 us -> 0 us
  between operations: 14.9 us -> 0.66 us
    psum x1 -> x0, waiting for transfers between devices: 55.8 us -> none  [shards(): lax.psum((local_kernel, gamma_local, beta_local), 'space')]
    ppermute x19 -> x0, starting transfers between devices: 49.2 us -> none  [from_behind(): lax.ppermute(value, axis, [(source, source + steps) for source in range(l...]
    slice x31 -> x0, local copies, waits for them, and re-layouts: 33.6 us -> none  [the longest x4 9.58 us: pull_lower(): sliver = field[..., span_z - 1::span_z]]
    psum x1 -> x0, blocking collectives: 28.4 us -> none  [shards(): lax.psum((local_kernel, gamma_local, beta_local), 'space')]
    pallas_call x0 -> x1, Pallas kernels: none -> 28.2 us  [shards(): pl.pallas_call(functools.partial(body, groups, scale), out_shape=(jax.Sha...]
    dot_general x31 -> x0, matrix products: 25.8 us -> none  [the longest x12 11.5 us: kernel_plane(): jnp.einsum('oxl,bcixl->obci', shifted_grad[shift_x, shift_y, shift_z], st...]
    reshape x10 -> x0, local copies, waits for them, and re-layouts: 10.3 us -> none  [the longest x4 4.8 us: pull_lower(): spread = jnp.repeat(arrived, span_z, axis=field.ndim - 1)]
    concatenate x13 -> x0, other arithmetic: 7.98 us -> none  [the longest x4 2.66 us: pull_lower(): return jnp.concatenate([arrived, field[..., :-1, :]], axis=field.ndim - 2)]
  transfers between devices with their start and end apart: 20 -> 0, of which waited for: 3 -> 0; matrix products, arithmetic and copies ran while one was open for 30% -> 0% of each run, Pallas kernels for 0% -> 0%
where the time goes in v1:
time: 37.9 us; the launch traced here: 37.6 us
  Pallas kernels  28.2 us (74%)
  local copies, waits for them, and re-layouts  8.73 us (23%)
  between operations  0.66 us (2%)
    pallas_call x1, Pallas kernels, shards(): pl.pallas_call(functools.partial(body, groups, scale), out_shape=(jax.Sha...  28.2 us
    unnamed x15, local copies, waits for them, and re-layouts  8.73 us

profile of v1, /device:TPU:0, one launch (start us, length us, event | category | flops | bytes accessed | tf_op | source)
XLA Modules:
  0.0 37.6 jit_solution(2220088855750664311)
XLA Ops:
  0.6 0.0 copy-start
  0.6 1.4 %copy-done = bf16[8,96,8,128]{3,2,1,0:T(8,128)(2,1)S(1)} copy-done((bf16[8,96,8,128]{3,2,1,0:T(8,128)(2,1)S(1)}, bf16[8,96,8,128]{3,2,1,0:T(8,128)(2,1)}, u32[]{:S(2)}) %copy-start) | copy-done | bytes 1572888
  2.0 0.0 copy-start.1
  2.0 1.0 %copy-done.1 = bf16[96,2592]{1,0:T(8,128)(2,1)S(1)} copy-done((bf16[96,2592]{1,0:T(8,128)(2,1)S(1)}, bf16[96,2592]{1,0:T(8,128)(2,1)}, u32[]{:S(2)}) %copy-start.1) | copy-done | bytes 497688
  3.1 0.0 copy-start.2
  3.1 0.9 %copy-done.2 = bf16[1,96,8,128]{3,2,1,0:T(8,128)(2,1)S(1)} copy-done((bf16[1,96,8,128]{3,2,1,0:T(8,128)(2,1)S(1)}, bf16[1,96,8,128]{3,2,1,0:T(8,128)(2,1)}, u32[]{:S(2)}) %copy-start.2) | copy-done | bytes 196632
  4.0 0.0 copy-start.3
  4.0 0.8 %copy-done.3 = f32[96,96]{1,0:T(8,128)S(1)} copy-done((f32[96,96]{1,0:T(8,128)S(1)}, f32[96,96]{1,0:T(8,128)}, u32[]{:S(2)}) %copy-start.3) | copy-done | bytes 36888
  4.8 0.0 copy-start.4
  4.8 0.7 %copy-done.4 = f32[96]{0:T(128)S(1)} copy-done((f32[96]{0:T(128)S(1)}, f32[96]{0:T(128)}, u32[]{:S(2)}) %copy-start.4) | copy-done | bytes 408
  5.5 28.2 %shard_map.92 = (bf16[1,96,8,128]{3,2,1,0:T(8,128)(2,1)S(1)}, bf16[8,96,8,128]{3,2,1,0:T(8,128)(2,1)S(1)}, f32[96,2592]{1,0:T(8,128)S(1)}, f32[96,96]{1,0:T(8,128)S(1)}, f32[1,96]{1,0:T(1,128)S(1)}) custom-call(bf16[8,96,8,128]{3,2,1,0:T(8,128)(2,1)S(1)} %copy-done, bf16[96,2592]{1,0:T(8,128)(2,1)S(1)} %copy-done.1, f32[1,96]{1,0:T(1,128)S(1)} %bitcast.2, ...), custom_call_target="tpu_custom_call" | custom-call | tf_op jit(solution)/shard_map/pallas_call | solution.py:461
  33.7 0.7 %copy.15 = bf16[1,96,8,128]{3,2,1,0:T(8,128)(2,1)} copy(bf16[1,96,8,128]{3,2,1,0:T(8,128)(2,1)S(1)} %get-tuple-element.20) | data formatting | bytes 393216
  34.4 1.1 %copy.16 = bf16[8,96,8,128]{3,2,1,0:T(8,128)(2,1)} copy(bf16[8,96,8,128]{3,2,1,0:T(8,128)(2,1)S(1)} %get-tuple-element.21) | data formatting | bytes 3145728
  35.5 1.0 %copy.17 = f32[96,2592]{1,0:T(8,128)} copy(f32[96,2592]{1,0:T(8,128)S(1)} %get-tuple-element.22) | data formatting | bytes 1990656
  36.5 0.6 %copy.18 = f32[96,96]{1,0:T(8,128)} copy(f32[96,96]{1,0:T(8,128)S(1)} %get-tuple-element.23) | data formatting | bytes 73728
  37.1 0.5 %copy.19 = f32[96]{0:T(128)} copy(f32[96]{0:T(128)S(1)} %bitcast.3) | data formatting | bytes 768
Async XLA Ops:
  0.6 1.4 %copy-start = (bf16[8,96,8,128]{3,2,1,0:T(8,128)(2,1)S(1)}, bf16[8,96,8,128]{3,2,1,0:T(8,128)(2,1)}, u32[]{:S(2)}) copy-start(bf16[8,96,8,128]{3,2,1,0:T(8,128)(2,1)} %vol.1) | copy-start | bytes 4718596
  2.0 1.0 %copy-start.1 = (bf16[96,2592]{1,0:T(8,128)(2,1)S(1)}, bf16[96,2592]{1,0:T(8,128)(2,1)}, u32[]{:S(2)}) copy-start(bf16[96,2592]{1,0:T(8,128)(2,1)} %ker.1) | copy-start | bytes 1492996
  3.1 0.9 %copy-start.2 = (bf16[1,96,8,128]{3,2,1,0:T(8,128)(2,1)S(1)}, bf16[1,96,8,128]{3,2,1,0:T(8,128)(2,1)}, u32[]{:S(2)}) copy-start(bf16[1,96,8,128]{3,2,1,0:T(8,128)(2,1)} %cot.1) | copy-start | bytes 589828
  4.0 0.8 %copy-start.3 = (f32[96,96]{1,0:T(8,128)S(1)}, f32[96,96]{1,0:T(8,128)}, u32[]{:S(2)}) copy-start(f32[96,96]{1,0:T(8,128)} %gamma.1) | copy-start | bytes 110596
  4.8 0.7 %copy-start.4 = (f32[96]{0:T(128)S(1)}, f32[96]{0:T(128)}, u32[]{:S(2)}) copy-start(f32[96]{0:T(128)} %param.7) | copy-start | bytes 1156

commit v2 on v1

--- a/solution.py
+++ b/solution.py
@@ -15,6 +15,7 @@
 LANES = 128
 SZ = 16
 ROWS = 9 * C
+DEPTH = 1024
 MESH = pl.DeviceIdType.MESH
 
 
@@ -30,11 +31,11 @@
     return pl.ds(x * LANES, LANES)
 
 
-def body(groups, scale, vol, ker, beta, gamma, cot, norm_o, dvol_o, kg_o, gg_o, bg_o,
-         tmp, V, Yp, Zp, Yr, Zr, Cr, Kf, WB, Gs, up, S, GY, GZ, GYr, GZr, GCr,
-         part, sendA, recvA, sendB, recvB, full, gacc, bacc,
+def body(groups, scale, vol_h, ker_h, beta_h, gamma_h, cot_h, norm_h, dvol_h, full_h,
+         norm_o, dvol_o, full, out_sem, vol, ker, beta, gamma, cot, tmp, V, Yp, Zp, Yr, Zr, Cr, Kf, WB, Gs, up, S, GY, GZ, GYr, GZr, GCr,
+         part, gslab, sendA, recvA, sendB, recvB, gacc, bacc, in_sem,
          ysend, yrecv, zsend, zrecv, csend, crecv, xsend, xrecv,
-         asend, arecv, bsend, brecv, gsend, grecv, dsend, drecv):
+         asend, arecv, bsend, brecv, gsend, grecv, dsend, drecv, esend, erecv):
     idx = lax.axis_index("space")
     gx = idx // 8
     by = idx // 2 % 4
@@ -43,6 +44,13 @@
 
     def dev(jy, jz):
         return {"space": base + jy * 2 + jz}
+
+    loads = [pltpu.make_async_copy(vol_h.at[pl.ds(4 * i, 4)], vol.at[pl.ds(4 * i, 4)], in_sem.at[i])
+             for i in range(2)]
+    loads += [pltpu.make_async_copy(src, dst, in_sem.at[2 + i]) for i, (src, dst) in enumerate(
+        ((ker_h, ker), (cot_h, cot), (gamma_h, gamma), (beta_h, beta)))]
+    for load in loads:
+        load.start()
 
     barrier = pltpu.get_barrier_semaphore()
     for k in range(1, 8):
@@ -89,6 +97,8 @@
                 Zp[px, py] = za.astype(BF)
         return 0
 
+    loads[0].wait()
+    loads[1].wait()
     lax.fori_loop(0, 2, spread_in, 0)
 
     pl.semaphore_wait(barrier, 7)
@@ -119,6 +129,8 @@
     def _():
         z_copy.start()
 
+    for load in loads[2:]:
+        load.wait()
     for tx in range(3):
         Kf[tx] = ker[:, tx * ROWS:(tx + 1) * ROWS]
     WB[...] = jnp.zeros_like(WB)
@@ -136,7 +148,8 @@
         Gs[v * LANES + C:(v + 1) * LANES, :] = jnp.zeros((LANES - C, 9 * LANES), BF)
     if groups == 1:
         Gs[:, 8 * LANES:] = jnp.zeros((4 * LANES, LANES), BF)
-        V[1, :, 0:LANES] = jnp.zeros((ROWS, LANES), BF)
+        V[1, :, 0:LANES] = jnp.zeros((DEPTH, LANES), BF)
+    V[:, ROWS:, :] = jnp.zeros((2, DEPTH - ROWS, 9 * LANES), BF)
     tmp[...] = cot[0].astype(F32).reshape(C * NX, LANES)
     for x in range(NX):
         up[:, tile(x)] = tmp[pl.ds(x, C, stride=NX), :]
@@ -211,7 +224,7 @@
 
         @pl.when(gx == 0)
         def _():
-            V[1, :, 0:LANES] = jnp.zeros((ROWS, LANES), BF)
+            V[1, :, 0:LANES] = jnp.zeros((DEPTH, LANES), BF)
 
     gacc[...] = jnp.zeros_like(gacc)
     bacc[...] = jnp.zeros_like(bacc)
@@ -219,9 +232,9 @@
     def forward(i, _):
         lo = pl.multiple_of(i * 256, 256)
         hi = pl.multiple_of(i * 256 + LANES, LANES)
-        conv = jnp.dot(Kf[1], V[0, :, pl.ds(hi, 256)], preferred_element_type=F32)
-        conv += jnp.dot(Kf[0], V[1, :, pl.ds(lo, 256)], preferred_element_type=F32)
-        conv += jnp.dot(Kf[2], V[1, :, pl.ds(hi, 256)], preferred_element_type=F32)
+        conv = jnp.dot(Kf[1], V[0, 0:ROWS, pl.ds(hi, 256)], preferred_element_type=F32)
+        conv += jnp.dot(Kf[0], V[1, 0:ROWS, pl.ds(lo, 256)], preferred_element_type=F32)
+        conv += jnp.dot(Kf[2], V[1, 0:ROWS, pl.ds(hi, 256)], preferred_element_type=F32)
         sq = conv * conv
         sq_b = sq.astype(BF)
         r = lax.rsqrt(beta_col + jnp.dot(gam_b, sq_b, preferred_element_type=F32))
@@ -240,6 +253,8 @@
 
     lax.fori_loop(0, 4, forward, 0)
     norm_o[0] = tmp[...].reshape(C, NX, LANES).astype(BF)
+    stores = [pltpu.make_async_copy(norm_o, norm_h, out_sem.at[0])]
+    stores[0].start()
 
     ya = jnp.zeros((C, LANES), F32)
     za = jnp.zeros((C, LANES), F32)
@@ -266,32 +281,53 @@
         gz_copy.start()
 
     nt = (((1,), (1,)), ((), ()))
-    for tx in range(3):
-        first = 0 if tx == 0 else LANES
-        plane = 0 if tx == 1 else 1
-        for s in range(4):
-            n = min(256, ROWS - s * 256)
-            k = lax.dot_general(Gs[0:C, 0:8 * LANES],
-                                V[plane, s * 256:s * 256 + n, first:first + 8 * LANES],
-                                nt, preferred_element_type=F32) * scale
-            if n == 256:
-                part[tx * 7 + s * 2] = k[:, :LANES]
-                part[tx * 7 + s * 2 + 1] = k[:, LANES:]
-            else:
-                part[tx * 7 + s * 2] = jnp.concatenate([k, jnp.zeros((C, LANES - C), F32)], axis=1)
     bsum = jnp.sum(bacc[...], axis=1, keepdims=True) * scale
-    part[21] = jnp.concatenate(
+    gslab[...] = jnp.concatenate(
         [gacc[...] * scale, jnp.broadcast_to(bsum, (C, LANES - C))], axis=1)
-    part[22] = jnp.zeros((C, LANES), F32)
-    part[23] = jnp.zeros((C, LANES), F32)
-
-    def to_a(i, _):
-        sendA[i] = part[(1 - bz) * 12 + i].astype(BF)
+
+    def slabs(pair):
+        tx = pair // 4
+        row = pl.multiple_of(pair % 4 * 256, 256)
+        first = pl.multiple_of((tx + 1) // 2 * LANES, LANES)
+        k = lax.dot_general(Gs[0:C, 0:8 * LANES],
+                            V[(tx + 1) % 2, pl.ds(row, 256), pl.ds(first, 8 * LANES)],
+                            nt, preferred_element_type=F32) * scale
+        return k[:, :LANES], k[:, LANES:] + jnp.where(pair == 11, gslab[...], 0.0)
+
+    def a_copy(i):
+        return remote(sendA.at[pl.ds(2 * i, 2)], recvA.at[pl.ds(2 * i, 2)], asend.at[i], arecv.at[i],
+                      dev(by, 1 - bz))
+
+    def theirs(i, _):
+        low, high = slabs((1 - bz) * 6 + i)
+        sendA[2 * i] = low.astype(BF)
+        sendA[2 * i + 1] = high.astype(BF)
+        a_copy(i).start()
         return 0
 
-    lax.fori_loop(0, 12, to_a, 0)
-    a_copy = remote(sendA, recvA, asend, arecv, dev(by, 1 - bz))
-    a_copy.start()
+    lax.fori_loop(0, 6, theirs, 0)
+
+    def ours(i, _):
+        low, high = slabs(bz * 6 + i)
+        part[2 * i] = low
+        part[2 * i + 1] = high
+        return 0
+
+    lax.fori_loop(0, 6, ours, 0)
+
+    def wait_a(i, _):
+        a_copy(i).wait()
+        return 0
+
+    lax.fori_loop(0, 6, wait_a, 0)
+    b_copy = []
+    for k in (2, 1, 3):
+        to = (by + k) % 4
+        for i in range(3):
+            j = to * 3 + i
+            sendB[k, i] = (part[j] + recvA[j].astype(F32)).astype(BF)
+        b_copy.append(remote(sendB.at[k], recvB.at[k], bsend.at[k], brecv.at[k], dev(to, bz)))
+        b_copy[-1].start()
 
     @pl.when(by < 3)
     def _():
@@ -344,22 +380,6 @@
         @pl.when(gx == groups - 1)
         def _():
             Gs[:, 8 * LANES:] = jnp.zeros((4 * LANES, LANES), BF)
-
-    a_copy.wait()
-
-    def add_a(i, _):
-        j = bz * 12 + i
-        total = part[j] + recvA[i].astype(F32)
-        part[j] = total
-        sendB[i // 3, i % 3] = total.astype(BF)
-        return 0
-
-    lax.fori_loop(0, 12, add_a, 0)
-    b_copy = []
-    for k in range(1, 4):
-        to = (by + k) % 4
-        b_copy.append(remote(sendB.at[to], recvB.at[k], bsend.at[k], brecv.at[k], dev(to, bz)))
-        b_copy[-1].start()
 
     def back(px):
         def step(i, _):
@@ -379,76 +399,117 @@
         lax.fori_loop(0, 4, step, 0)
         for q in range(4):
             dvol_o[px * 4 + q] = S[q * C * NX:(q + 1) * C * NX].reshape(C, NX, LANES).astype(BF)
+        stores.append(pltpu.make_async_copy(
+            dvol_o.at[pl.ds(4 * px, 4)], dvol_h.at[pl.ds(4 * px, 4)], out_sem.at[1 + px]))
+        stores[-1].start()
 
     back(0)
 
     for c in b_copy:
         c.wait()
     for i in range(3):
-        total = part[bz * 12 + by * 3 + i]
+        total = part[by * 3 + i] + recvA[by * 3 + i].astype(F32)
         for k in range(1, 4):
             total += recvB[k, i].astype(F32)
         full[bz, by, i] = total.astype(BF)
     d_copy = []
-    for k in range(1, 4):
+    for k in (2, 1, 3):
         to = (by + k) % 4
         d_copy.append(remote(full.at[bz, by], full.at[bz, by], dsend.at[k], drecv.at[k], dev(to, bz)))
         d_copy[-1].start()
 
+    def e_copy(half, k):
+        source = (by + 4 - k) % 4
+        return remote(full.at[half, source], full.at[half, source], esend.at[k], erecv.at[k],
+                      dev(by, 1 - bz))
+
+    e_copy(bz, 0).start()
+
     back(1)
 
-    for k in range(1, 4):
+    for k in (1, 3, 2):
         source = (by + 4 - k) % 4
         remote(full.at[bz, source], full.at[bz, source], dsend.at[k], drecv.at[k],
-               dev((by + k) % 4, bz)).wait()
-    e_copy = remote(full.at[bz], full.at[bz], dsend.at[0], drecv.at[0], dev(by, 1 - bz))
-    e_copy.start()
-    e_copy.wait_send()
-    remote(full.at[1 - bz], full.at[1 - bz], dsend.at[0], drecv.at[0], dev(by, 1 - bz)).wait_recv()
-
+               dev((by + k) % 4, bz)).wait_recv()
+        e_copy(bz, k).start()
+    for k in range(4):
+        e_copy(1 - bz, k).wait_recv()
+        e_copy(bz, k).wait_send()
+    for d in d_copy:
+        d.wait_send()
+
+    stores.append(pltpu.make_async_copy(full, full_h, out_sem.at[3]))
+    stores[-1].start()
+    for store in stores:
+        store.wait()
+
+    @pl.when(by < 3)
+    def _():
+        y_copy.wait_send()
+
+        @pl.when(bz == 0)
+        def _():
+            for c in c_copy:
+                c.wait_send()
+
+    @pl.when(bz == 0)
+    def _():
+        z_copy.wait_send()
+
+    @pl.when(by > 0)
+    def _():
+        gy_copy.wait_send()
+
+        @pl.when(bz == 1)
+        def _():
+            gc_copy.wait_send()
+
+    @pl.when(bz == 1)
+    def _():
+        gz_copy.wait_send()
+
+    if groups > 1:
+        @pl.when(gx < groups - 1)
+        def _():
+            x_copy.wait_send()
+
+        @pl.when(gx > 0)
+        def _():
+            h_copy.wait_send()
+
+
+def finish(norm, dvol, full_h, norm_o, dvol_o, kg_o, gg_o, bg_o, full, kg, gg, bg, norm_v, dvol_v, sem):
+    load = pltpu.make_async_copy(full_h, full, sem.at[5])
+    load.start()
+    fetch = [pltpu.make_async_copy(dvol.at[pl.ds(2 * i, 2)], dvol_v.at[pl.ds(2 * i, 2)], sem.at[6 + i])
+             for i in range(4)]
+    fetch.append(pltpu.make_async_copy(norm, norm_v, sem.at[10]))
+    for f in fetch:
+        f.start()
+    copies = [pltpu.make_async_copy(dvol_v, dvol_o, sem.at[0]), pltpu.make_async_copy(norm_v, norm_o, sem.at[1])]
+    for f in fetch:
+        f.wait()
+    for c in copies:
+        c.start()
+    load.wait()
     for tx in range(3):
         for s in range(7):
-            j = tx * 7 + s
+            j = tx * 8 + s
             n = min(LANES, ROWS - s * LANES)
             at = tx * ROWS + s * LANES
-            kg_o[:, at:at + n] = full[j // 12, j % 12 // 3, j % 3][:, :n].astype(F32)
-    last = full[1, 3, 0].astype(F32)
-    gg_o[...] = last[:, :C]
-    bg_o[...] = jnp.sum(jnp.where(eye, last[:, C:C + 1], 0.0), axis=0, keepdims=True)
-
-    @pl.when(by < 3)
-    def _():
-        y_copy.wait_send()
-
-        @pl.when(bz == 0)
-        def _():
-            for c in c_copy:
-                c.wait_send()
-
-    @pl.when(bz == 0)
-    def _():
-        z_copy.wait_send()
-
-    @pl.when(by > 0)
-    def _():
-        gy_copy.wait_send()
-
-        @pl.when(bz == 1)
-        def _():
-            gc_copy.wait_send()
-
-    @pl.when(bz == 1)
-    def _():
-        gz_copy.wait_send()
-
-    if groups > 1:
-        @pl.when(gx < groups - 1)
-        def _():
-            x_copy.wait_send()
-
-        @pl.when(gx > 0)
-        def _():
-            h_copy.wait_send()
+            kg[:, at:at + n] = full[j // 12, j % 12 // 3, j % 3][:, :n].astype(F32)
+    copies.append(pltpu.make_async_copy(kg, kg_o, sem.at[2]))
+    copies[-1].start()
+    last = full[1, 3, 2].astype(F32)
+    eye = (lax.broadcasted_iota(jnp.int32, (C, C), 0) == lax.broadcasted_iota(jnp.int32, (C, C), 1))
+    gg[...] = last[:, :C]
+    bg[...] = jnp.sum(jnp.where(eye, last[:, C:C + 1], 0.0), axis=0, keepdims=True)
+    copies.append(pltpu.make_async_copy(gg, gg_o, sem.at[3]))
+    copies.append(pltpu.make_async_copy(bg, bg_o, sem.at[4]))
+    copies[3].start()
+    copies[4].start()
+    for c in copies:
+        c.wait()
 
 
 def shards(volume, kernel, beta, gamma, cotangent):
@@ -457,34 +518,48 @@
     scale = 1.0 / math.sqrt(NX * LANES * devices)
     vm = lambda *shape, dtype=BF: pltpu.VMEM(shape, dtype)
     dma = lambda *shape: pltpu.SemaphoreType.DMA(shape) if shape else pltpu.SemaphoreType.DMA
-    spec = pl.BlockSpec(memory_space=pltpu.VMEM)
-    out = pl.pallas_call(
+    hbm = pl.BlockSpec(memory_space=pltpu.HBM)
+    norm, dvol, full = pl.pallas_call(
         functools.partial(body, groups, scale),
         out_shape=(
             jax.ShapeDtypeStruct((1, C, NX, LANES), BF),
             jax.ShapeDtypeStruct((8, C, NX, LANES), BF),
+            jax.ShapeDtypeStruct((2, 4, 3, C, LANES), BF),
+        ),
+        in_specs=[hbm] * 5,
+        out_specs=(hbm,) * 3,
+        scratch_shapes=[
+            vm(1, C, NX, LANES), vm(8, C, NX, LANES), vm(2, 4, 3, C, LANES), dma(4),
+            vm(8, C, NX, LANES), vm(C, 27 * C), vm(1, C, dtype=F32), vm(C, C, dtype=F32), vm(1, C, NX, LANES),
+            vm(C * NX, LANES, dtype=F32), vm(2, DEPTH, 9 * LANES),
+            vm(2, 2, C, LANES), vm(2, 2, C, LANES), vm(2, 2, C, LANES), vm(2, 2, C, LANES), vm(2, C, LANES),
+            vm(3, C, ROWS), vm(3, 4 * C, 4 * LANES), vm(4 * LANES, 9 * LANES),
+            vm(C, NX * LANES, dtype=F32), vm(4 * C * NX, LANES, dtype=F32),
+            vm(C, LANES), vm(C, LANES), vm(C, LANES), vm(C, LANES), vm(C, LANES),
+            vm(12, C, LANES, dtype=F32), vm(C, LANES, dtype=F32), vm(12, C, LANES), vm(12, C, LANES),
+            vm(4, 3, C, LANES), vm(4, 3, C, LANES),
+            vm(C, C, dtype=F32), vm(C, LANES, dtype=F32), dma(6),
+            dma(), dma(), dma(), dma(), dma(2), dma(2), dma(2), dma(2),
+            dma(6), dma(6), dma(4), dma(4), dma(3), dma(3), dma(4), dma(4), dma(4), dma(4),
+        ],
+        compiler_params=pltpu.CompilerParams(
+            collective_id=0, has_side_effects=True, vmem_limit_bytes=58 * 1024 * 1024),
+    )(volume, kernel, beta.reshape(1, C), gamma, cotangent)
+    normalized, dvol, kg, gg, bg = pl.pallas_call(
+        finish,
+        out_shape=(
+            jax.ShapeDtypeStruct(norm.shape, BF),
+            jax.ShapeDtypeStruct(dvol.shape, BF),
             jax.ShapeDtypeStruct((C, 27 * C), F32),
             jax.ShapeDtypeStruct((C, C), F32),
             jax.ShapeDtypeStruct((1, C), F32),
         ),
-        in_specs=[spec] * 5,
-        out_specs=(spec,) * 5,
-        scratch_shapes=[
-            vm(C * NX, LANES, dtype=F32), vm(2, ROWS, 9 * LANES),
-            vm(2, 2, C, LANES), vm(2, 2, C, LANES), vm(2, 2, C, LANES), vm(2, 2, C, LANES), vm(2, C, LANES),
-            vm(3, C, ROWS), vm(3, 4 * C, 4 * LANES), vm(4 * LANES, 9 * LANES),
-            vm(C, NX * LANES, dtype=F32), vm(4 * C * NX, LANES, dtype=F32),
-            vm(C, LANES), vm(C, LANES), vm(C, LANES), vm(C, LANES), vm(C, LANES),
-            vm(24, C, LANES, dtype=F32), vm(12, C, LANES), vm(12, C, LANES),
-            vm(4, 3, C, LANES), vm(4, 3, C, LANES), vm(2, 4, 3, C, LANES),
-            vm(C, C, dtype=F32), vm(C, LANES, dtype=F32),
-            dma(), dma(), dma(), dma(), dma(2), dma(2), dma(2), dma(2),
-            dma(), dma(), dma(4), dma(4), dma(3), dma(3), dma(4), dma(4),
-        ],
-        compiler_params=pltpu.CompilerParams(
-            collective_id=0, has_side_effects=True, vmem_limit_bytes=48 * 1024 * 1024),
-    )(volume, kernel, beta.reshape(1, C), gamma, cotangent)
-    normalized, dvol, kg, gg, bg = out
+        in_specs=[hbm] * 3,
+        out_specs=(hbm,) * 5,
+        scratch_shapes=[vm(2, 4, 3, C, LANES), vm(C, 27 * C, dtype=F32), vm(C, C, dtype=F32),
+                        vm(1, C, dtype=F32), vm(1, C, NX, LANES), vm(8, C, NX, LANES), dma(11)],
+        compiler_params=pltpu.CompilerParams(vmem_limit_bytes=58 * 1024 * 1024),
+    )(norm, dvol, full)
     if groups > 1:
         kg, gg, bg = jax.tree.map(lambda a: a * 0.125, lax.psum((kg, gg, bg), "space"))
     return normalized, dvol, kg, gg, bg.reshape(C)

time: 37.9 us -> 34.4 us (0.908)
  local copies, waits for them, and re-layouts: 8.73 us -> 0 us
  Pallas kernels: 28.2 us -> 33.6 us
    unnamed x15 -> x0, local copies, waits for them, and re-layouts: 8.73 us -> none
    pallas_call x0 -> x1, Pallas kernels: none -> 3.22 us  [shards(): pl.pallas_call(finish, out_shape=(jax.ShapeDtypeStruct(norm.shape, BF), j...]
    pallas_call x1, Pallas kernels: 28.2 us -> 30.4 us  [shards(): pl.pallas_call(functools.partial(body, groups, scale), out_shape=(jax.Sha...]
where the time goes in v2:
time: 34.4 us; the launch traced here: 34.3 us
  Pallas kernels  33.6 us (98%)
  between operations  0.64 us (2%)
    pallas_call x1, Pallas kernels, shards(): pl.pallas_call(functools.partial(body, groups, scale), out_shape=(jax.Sha...  30.4 us
    pallas_call x1, Pallas kernels, shards(): pl.pallas_call(finish, out_shape=(jax.ShapeDtypeStruct(norm.shape, BF), j...  3.22 us

profile of v2, /device:TPU:0, one launch (start us, length us, event | category | flops | bytes accessed | tf_op | source)
XLA Modules:
  0.0 34.3 jit_solution(8438188008831842443)
XLA Ops:
  0.6 30.4 %shard_map.92 = (bf16[1,96,8,128]{3,2,1,0:T(8,128)(2,1)}, bf16[8,96,8,128]{3,2,1,0:T(8,128)(2,1)}, bf16[2,4,3,96,128]{4,3,2,1,0:T(8,128)(2,1)}) custom-call(bf16[8,96,8,128]{3,2,1,0:T(8,128)(2,1)} %vol_h.1, bf16[96,2592]{1,0:T(8,128)(2,1)} %ker_h.1, f32[1,96]{1,0:T(1,128)} %bitcast.2, f32[96,96]{1,0:T(8,128)} %gamma_h.1, bf16[1,96,8,128]{3,2,1,0:T(8,128)(2,1)} %cot_h.1), custom_call_target="tpu_custom_call" | custom-call | tf_op jit(solution)/shard_map/pallas_call | solution.py:522
  31.0 3.2 %shard_map.93 = (bf16[1,96,8,128]{3,2,1,0:T(8,128)(2,1)}, bf16[8,96,8,128]{3,2,1,0:T(8,128)(2,1)}, f32[96,2592]{1,0:T(8,128)}, f32[96,96]{1,0:T(8,128)}, f32[1,96]{1,0:T(1,128)}) custom-call(bf16[1,96,8,128]{3,2,1,0:T(8,128)(2,1)} %get-tuple-element.13.norm, bf16[8,96,8,128]{3,2,1,0:T(8,128)(2,1)} %get-tuple-element.14.dvol, ...), custom_call_target="tpu_custom_call" | custom-call | tf_op jit(solution)/shard_map/pallas_call | solution.py:548

commit v3 on v2

--- a/solution.py
+++ b/solution.py
@@ -78,8 +78,8 @@
             src_ref=src, dst_ref=dst, send_sem=ss, recv_sem=rs,
             device_id=target, device_id_type=MESH)
 
-    def spread_in(px, _):
-        for py, pz in ((1, 1), (1, 0), (0, 1), (0, 0)):
+    def spread_in(parities, px, _):
+        for py, pz in parities:
             r = row_of(1 + py, 1 + pz)
             tmp[...] = vol[px * 4 + py * 2 + pz].astype(F32).reshape(C * NX, LANES)
             ya = jnp.zeros((C, LANES), F32)
@@ -99,7 +99,7 @@
 
     loads[0].wait()
     loads[1].wait()
-    lax.fori_loop(0, 2, spread_in, 0)
+    lax.fori_loop(0, 2, functools.partial(spread_in, ((1, 1), (1, 0), (0, 1))), 0)
 
     pl.semaphore_wait(barrier, 7)
     if groups > 1:
@@ -129,6 +129,7 @@
     def _():
         z_copy.start()
 
+    lax.fori_loop(0, 2, functools.partial(spread_in, ((0, 0),)), 0)
     for load in loads[2:]:
         load.wait()
     for tx in range(3):
@@ -298,7 +299,10 @@
         return remote(sendA.at[pl.ds(2 * i, 2)], recvA.at[pl.ds(2 * i, 2)], asend.at[i], arecv.at[i],
                       dev(by, 1 - bz))
 
-    def theirs(i, _):
+    away = (by // 2 + 1) % 2
+
+    def theirs(step, _):
+        i = (step + 3 * away) % 6
         low, high = slabs((1 - bz) * 6 + i)
         sendA[2 * i] = low.astype(BF)
         sendA[2 * i + 1] = high.astype(BF)
@@ -313,21 +317,19 @@
         part[2 * i + 1] = high
         return 0
 
-    lax.fori_loop(0, 6, ours, 0)
-
-    def wait_a(i, _):
-        a_copy(i).wait()
-        return 0
-
-    lax.fori_loop(0, 6, wait_a, 0)
     b_copy = []
-    for k in (2, 1, 3):
-        to = (by + k) % 4
+    for step in range(2):
+        half = (away + step) % 2
+        lax.fori_loop(3 * half, 3 * half + 3, ours, 0)
         for i in range(3):
-            j = to * 3 + i
-            sendB[k, i] = (part[j] + recvA[j].astype(F32)).astype(BF)
-        b_copy.append(remote(sendB.at[k], recvB.at[k], bsend.at[k], brecv.at[k], dev(to, bz)))
-        b_copy[-1].start()
+            a_copy(3 * half + i).wait()
+        for to in ((2 * half, 2 * half + 1) if step == 0 else (2 * half + 1 - by % 2,)):
+            k = (to + 4 - by) % 4
+            for i in range(3):
+                j = to * 3 + i
+                sendB[k, i] = (part[j] + recvA[j].astype(F32)).astype(BF)
+            b_copy.append(remote(sendB.at[k], recvB.at[k], bsend.at[k], brecv.at[k], dev(to, bz)))
+            b_copy[-1].start()
 
     @pl.when(by < 3)
     def _():
@@ -486,11 +488,7 @@
     fetch.append(pltpu.make_async_copy(norm, norm_v, sem.at[10]))
     for f in fetch:
         f.start()
-    copies = [pltpu.make_async_copy(dvol_v, dvol_o, sem.at[0]), pltpu.make_async_copy(norm_v, norm_o, sem.at[1])]
-    for f in fetch:
-        f.wait()
-    for c in copies:
-        c.start()
+    copies = []
     load.wait()
     for tx in range(3):
         for s in range(7):
@@ -500,14 +498,22 @@
             kg[:, at:at + n] = full[j // 12, j % 12 // 3, j % 3][:, :n].astype(F32)
     copies.append(pltpu.make_async_copy(kg, kg_o, sem.at[2]))
     copies[-1].start()
+    for i in range(4):
+        fetch[i].wait()
+        copies.append(pltpu.make_async_copy(
+            dvol_v.at[pl.ds(2 * i, 2)], dvol_o.at[pl.ds(2 * i, 2)], sem.at[11 + i]))
+        copies[-1].start()
+    fetch[4].wait()
+    copies.append(pltpu.make_async_copy(norm_v, norm_o, sem.at[1]))
+    copies[-1].start()
     last = full[1, 3, 2].astype(F32)
     eye = (lax.broadcasted_iota(jnp.int32, (C, C), 0) == lax.broadcasted_iota(jnp.int32, (C, C), 1))
     gg[...] = last[:, :C]
     bg[...] = jnp.sum(jnp.where(eye, last[:, C:C + 1], 0.0), axis=0, keepdims=True)
     copies.append(pltpu.make_async_copy(gg, gg_o, sem.at[3]))
     copies.append(pltpu.make_async_copy(bg, bg_o, sem.at[4]))
-    copies[3].start()
-    copies[4].start()
+    copies[-2].start()
+    copies[-1].start()
     for c in copies:
         c.wait()
 
@@ -557,7 +563,7 @@
         in_specs=[hbm] * 3,
         out_specs=(hbm,) * 5,
         scratch_shapes=[vm(2, 4, 3, C, LANES), vm(C, 27 * C, dtype=F32), vm(C, C, dtype=F32),
-                        vm(1, C, dtype=F32), vm(1, C, NX, LANES), vm(8, C, NX, LANES), dma(11)],
+                        vm(1, C, dtype=F32), vm(1, C, NX, LANES), vm(8, C, NX, LANES), dma(15)],
         compiler_params=pltpu.CompilerParams(vmem_limit_bytes=58 * 1024 * 1024),
     )(norm, dvol, full)
     if groups > 1:

time: 34.4 us -> 32.4 us (0.942)
  Pallas kernels: 33.6 us -> 31.6 us
    pallas_call x1, Pallas kernels: 30.4 us -> 28.7 us  [shards(): pl.pallas_call(functools.partial(body, groups, scale), out_shape=(jax.Sha...]
where the time goes in v3:
time: 32.4 us; the launch traced here: 32.2 us
  Pallas kernels  31.6 us (98%)
  between operations  0.64 us (2%)
    pallas_call x1, Pallas kernels, shards(): pl.pallas_call(functools.partial(body, groups, scale), out_shape=(jax.Sha...  28.7 us
    pallas_call x1, Pallas kernels, shards(): pl.pallas_call(finish, out_shape=(jax.ShapeDtypeStruct(norm.shape, BF), j...  2.92 us

profile of v3, /device:TPU:0, one launch (start us, length us, event | category | flops | bytes accessed | tf_op | source)
XLA Modules:
  0.0 32.2 jit_solution(6049516272921818847)
XLA Ops:
  0.6 28.7 %shard_map.92 = (bf16[1,96,8,128]{3,2,1,0:T(8,128)(2,1)}, bf16[8,96,8,128]{3,2,1,0:T(8,128)(2,1)}, bf16[2,4,3,96,128]{4,3,2,1,0:T(8,128)(2,1)}) custom-call(bf16[8,96,8,128]{3,2,1,0:T(8,128)(2,1)} %vol_h.1, bf16[96,2592]{1,0:T(8,128)(2,1)} %ker_h.1, f32[1,96]{1,0:T(1,128)} %bitcast.2, f32[96,96]{1,0:T(8,128)} %gamma_h.1, bf16[1,96,8,128]{3,2,1,0:T(8,128)(2,1)} %cot_h.1), custom_call_target="tpu_custom_call" | custom-call | tf_op jit(solution)/shard_map/pallas_call | solution.py:528
  29.3 2.9 %shard_map.93 = (bf16[1,96,8,128]{3,2,1,0:T(8,128)(2,1)}, bf16[8,96,8,128]{3,2,1,0:T(8,128)(2,1)}, f32[96,2592]{1,0:T(8,128)}, f32[96,96]{1,0:T(8,128)}, f32[1,96]{1,0:T(1,128)}) custom-call(bf16[1,96,8,128]{3,2,1,0:T(8,128)(2,1)} %get-tuple-element.13.norm, bf16[8,96,8,128]{3,2,1,0:T(8,128)(2,1)} %get-tuple-element.14.dvol, ...), custom_call_target="tpu_custom_call" | custom-call | tf_op jit(solution)/shard_map/pallas_call | solution.py:554
